TPU v7x, 32 devices: a whole 2x2x4 slice. The times are simulated.
32 devices in a mesh: work: 4 (over x, core), serv: 8 (over z, y).
Axes of the slice: x: 2, y: 2, z: 4, core: 2. Of those that a mesh axis runs over, the one named last changes fastest.
Arguments:
- user_factors: float32 [12288, 512], P(('work', 'serv')), may hold values from -6 to 6
- ratings: bfloat16 [12288, 8192], P(('work', 'serv')), may hold values from -6 to 6
- row_mask: int32 [12288, 16], P(('work', 'serv')), may hold values 0 or 1
- touched: int32 [32, 16], P(('work', 'serv')), may hold values from 0 to 31, as said below
- stale_cache: bfloat16 [262144, 512], P(('work', 'serv')), may hold values from -0.25 to 0.25
- item_factors: float32 [16384, 512], P('serv'), may hold values from -0.25 to 0.25
- roster: int32 [4], P('work'), may hold values from 0 to 7
Outputs:
- users_next: float32 [12288, 512], P(('work', 'serv'))
- items_next: float32 [16384, 512], P('serv')
Inputs may be any that keep to these rules, and one draw needn't show every extreme that they name: `touched`: each row holds 16 different blocks; a block's server is its number // 4; each server named in a row is named by exactly 2 of its entries, so 8 servers a row; every row of worker d = w * 8 + j names server roster[w].
All inputs are finite; a program needn't handle non-finite values. No bound on the sum of `row_mask` on one device may be relied on, other than what follows from the above.
Results may differ from a plain program's by a relative error of at most 0.004.
Values may be sent and summed in bfloat16 or wider, within the bound.
A program may use at most 256 MiB of HBM per device.

v0:
```python
import jax
import jax.numpy as jnp
from jax import lax
from jax.sharding import PartitionSpec as P

BPS = 4
CAP = 2


def broadcast(value, axis, root):
    mine = lax.axis_index(axis) == root
    return lax.psum(jnp.where(mine, value, jnp.zeros_like(value)), axis)


def shards(user_factors, ratings, row_mask, touched, stale_cache, item_factors, roster):
    servers = lax.axis_size("serv")
    rows_here = user_factors.shape[0]
    count = touched.shape[1]
    width = item_factors.shape[1]
    block = ratings.shape[1] // count
    fresh = broadcast(item_factors.astype(jnp.bfloat16), "serv", roster[0])
    fresh_blocks = fresh.reshape(BPS, block, width)
    ids = touched[0]
    owners = ids // BPS
    chosen = jnp.take(fresh_blocks, ids % BPS, axis=0)
    cached = stale_cache.reshape(count, block, width)
    used = jnp.where((owners == roster[0])[:, None, None], chosen, cached)
    user_b = user_factors.astype(jnp.bfloat16)
    pred = jnp.einsum("ur,kbr->ukb", user_b, used, preferred_element_type=jnp.float32)
    rate = ratings.reshape(rows_here, count, block)
    marks = row_mask.astype(jnp.float32)
    err = (marks[:, :, None] * (rate - pred)).astype(jnp.bfloat16)
    item_grad = jnp.einsum("ukb,ur->kbr", err, user_b, preferred_element_type=jnp.float32)
    user_grad = jnp.einsum("ukb,kbr->ur", err, used, preferred_element_type=jnp.float32)
    users_next = user_factors - 0.05 * (0.1 * user_factors - user_grad)
    order = jnp.arange(count, dtype=jnp.int32)
    same = (owners[:, None] == owners[None, :]) & (order[None, :] < order[:, None])
    rank_in = jnp.sum(same.astype(jnp.int32), axis=1)
    slot = owners * CAP + rank_in
    slots_all = jnp.arange(servers * CAP, dtype=jnp.int32)
    placing = slot[None, :] == slots_all[:, None]
    onehot = placing.astype(jnp.float32)
    slot_ids = jnp.sum(jnp.where(placing, ids[None, :] + 1, 0), axis=1) - 1
    mine_first = lax.axis_index("serv") * BPS
    local_blocks = mine_first + jnp.arange(BPS, dtype=jnp.int32)
    workers = lax.axis_size("work")
    piece = block // workers
    pieces = item_grad.reshape(count, workers, piece * width)
    sendbuf = jnp.einsum("sk,kwx->wsx", onehot, pieces, precision=lax.Precision.HIGHEST)
    sendbuf = sendbuf.reshape(workers * servers, CAP, piece * width)
    ids_all = jnp.broadcast_to(slot_ids.reshape(1, servers, CAP), (workers, servers, CAP)).reshape(
        workers * servers, CAP
    )
    received, rids = (
        lax.all_to_all(sendbuf, ("work", "serv"), split_axis=0, concat_axis=0, tiled=True),
        lax.all_to_all(ids_all, ("work", "serv"), split_axis=0, concat_axis=0, tiled=True),
    )
    select = (rids.reshape(1, -1) == local_blocks[:, None]).astype(jnp.float32)
    partial_sum = jnp.dot(
        select,
        received.reshape(workers * servers * CAP, piece * width),
        precision=lax.Precision.HIGHEST,
    )
    current = lax.dynamic_slice_in_dim(
        item_factors.reshape(BPS, workers, piece * width), lax.axis_index("work"), 1, 1
    )
    updated = current - 0.01 * (partial_sum[:, None, :] + 0.1 * current)
    whole = lax.all_gather(updated, "work", axis=1, tiled=True)
    items_next = whole.reshape(BPS * block, width)
    return (users_next, items_next)


def solution(mesh):
    in_specs = (
        P(("work", "serv"), None),
        P(("work", "serv"), None),
        P(("work", "serv"), None),
        P(("work", "serv"), None),
        P(("work", "serv"), None),
        P("serv", None),
        P("work"),
    )
    out_specs = (P(("work", "serv"), None), P("serv", None))
    return jax.shard_map(shards, mesh=mesh, in_specs=in_specs, out_specs=out_specs, check_vma=False)
```

profile of v0, /device:TPU:0, one launch (start us, length us, event | category | flops | bytes accessed | tf_op | source)
XLA Modules:
  0.0 672.5 jit_solution(6740958364335032703)
XLA Ops:
  7.9 3.7 convert_select_fusion
  11.7 0.2 convert_reduce_fusion
  12.1 0.6 broadcast_in_dim.59.clone
  12.7 7.3 %all-to-all-start = ((s32[32,1,2]{2,1,0:T(1,128)}), s32[32,1,2]{2,1,0:T(1,128)S(1)}, u32[]{:S(2)}, u32[]{:S(2)}) async-start(s32[32,1,2]{2,1,0:T(1,128)} %bitcast.14), calls=%async_computation | async-start | bytes 32768 | tf_op jit(solution)/shard_map/all_to_all | solution.py:56
  20.0 9.5 %copy.28 = f32[384,8192]{0,1:T(8,128)} copy(bf16[384,8192]{1,0:T(8,128)(2,1)} %param.8) | data formatting | bytes 18874368 | tf_op jit(solution)/shard_map/convert_element_type | solution.py:32
  29.6 87.4 %all-reduce.2.cloned.1.call-done = bf16[4,512,512]{2,1,0:T(8,128)(2,1)} async-done(((bf16[4,512,512]{2,1,0:T(8,128)(2,1)}), bf16[4,512,512]{2,1,0:T(8,128)(2,1)}) %all-reduce.2.cloned.1.call-update) | async-done | bytes 2097168 | tf_op jit(solution)/shard_map/psum | solution.py:12
  116.9 6.2 gather_fusion
  123.2 16.6 %fusion.5 = bf16[384,16,512]{0,2,1:T(8,128)(2,1)} fusion(f32[384,16,512]{0,2,1:T(8,128)} %bitcast.71, f32[384,16]{0,1:T(8,128)S(1)} %convert_element_type.23, f32[384,512]{1,0:T(8,128)S(1)} %copy-done, bf16[16,512,512]{2,1,0:T(8,128)(2,1)} %bitcast.73, bf16[16,512,512]{2,1,0:T(8,128)(2,1)} %gather_fusion, pred[16]{0:T(512)(128)(4,1)S(1)} %get-tuple-element.6, ...), kind=kOutput, calls=%fused_computation.9 | convolution fusion | flops 3239247872 | bytes 36462624 | tf_op jit(solution)/shard_map/ur,kbr->ukb/dot_general | solution.py:29
  139.8 11.0 %fusion.9 = f32[16,512,512]{2,1,0:T(8,128)} fusion(bf16[384,16,512]{0,2,1:T(8,128)(2,1)} %fusion.5, f32[384,512]{1,0:T(8,128)S(1)} %copy-done), kind=kOutput, calls=%fused_computation.16 | convolution fusion | flops 3221422080 | bytes 23855104 | tf_op jit(solution)/shard_map/ukb,ur->kbr/dot_general | solution.py:33
  150.9 20.5 %reshape.176 = f32[16,4,65536]{2,1,0:T(4,128)} reshape(f32[16,512,512]{2,1,0:T(8,128)} %fusion.9) | data formatting | bytes 33554432 | tf_op jit(solution)/shard_map/reshape | solution.py:48
  171.3 25.8 %convolution_bitcast_fusion = f32[4,16,65536]{2,1,0:T(8,128)} fusion(f32[16,4,65536]{2,1,0:T(4,128)} %reshape.176, s32[16]{0:T(128)S(1)} %fusion.23), kind=kOutput, calls=%fused_computation.1 | convolution fusion | flops 805306624 | bytes 33554496 | tf_op jit(solution)/shard_map/sk,kwx->wsx/dot_general | solution.py:49
  197.1 17.1 %reshape.177 = f32[32,2,65536]{2,1,0:T(2,128)} reshape(f32[4,16,65536]{2,1,0:T(8,128)} %convolution_bitcast_fusion) | data formatting | bytes 33554432 | tf_op jit(solution)/shard_map/reshape | solution.py:50
  214.2 4.5 all-to-all-start.1
  218.7 6.2 reshape.175
  225.0 3.3 constant_dynamic-slice_fusion
  228.2 0.5 broadcast.212
  228.7 0.7 reduce.3
  229.5 364.2 %all-to-all-done.1 = f32[32,2,65536]{2,1,0:T(2,128)} async-done(((f32[32,2,65536]{2,1,0:T(2,128)}), f32[32,2,65536]{2,1,0:T(2,128)}, u32[]{:S(2)}, u32[]{:S(2)}) %all-to-all-start.1) | async-done | bytes 16777248 | tf_op jit(solution)/shard_map/all_to_all | solution.py:55
  593.7 17.6 %reshape.178 = f32[64,65536]{1,0:T(8,128)} reshape(f32[32,2,65536]{2,1,0:T(2,128)} %all-to-all-done.1) | data formatting | bytes 33554432 | tf_op jit(solution)/shard_map/reshape | solution.py:61
  611.4 10.5 %fusion.2 = f32[4,1,65536]{2,0,1:T(4,128)} fusion(f32[64,65536]{1,0:T(8,128)} %reshape.178, f32[4,1,65536]{2,1,0:T(1,128)S(1)} %constant_dynamic-slice_fusion, s32[64]{0:T(128)S(1)} %eq.68, s32[4]{0:T(128)S(1)} %iota_add_fusion), kind=kOutput, calls=%fused_computation.5 | convolution fusion | flops 202375424 | bytes 18874640 | tf_op jit(solution)/shard_map/dot_general | solution.py:59
  621.8 13.4 %fusion.8 = f32[384,512]{1,0:T(8,128)} fusion(f32[384,512]{1,0:T(8,128)S(1)} %copy-done, bf16[384,16,512]{0,2,1:T(8,128)(2,1)} %fusion.5, bf16[16,512,512]{2,1,0:T(8,128)(2,1)} %bitcast.74, bf16[16,512,512]{2,1,0:T(8,128)(2,1)} %gather_fusion, pred[16]{0:T(512)(128)(4,1)S(1)} %get-tuple-element.6, pred[16]{0:T(512)(128)(4,1)S(1)} %get-tuple-element.2), kind=kOutput, calls=%fused_computation.15 | convolution fusion | flops 3230400512 | bytes 24641568 | tf_op jit(solution)/shard_map/ukb,kbr->ur/dot_general | solution.py:34
  635.3 17.5 %all-gather.2.cloned.1.call-done = f32[4,4,65536]{2,0,1:T(4,128)} async-done(((f32[4,1,65536]{2,0,1:T(4,128)}), f32[4,4,65536]{2,0,1:T(4,128)}) %all-gather.2.cloned.1.call-update) | async-done | bytes 4194320 | tf_op jit(solution)/shard_map/all_gather | solution.py:68
  652.7 6.9 %copy.34 = f32[4,4,65536]{2,1,0:T(4,128)} copy(f32[4,4,65536]{2,0,1:T(4,128)} %all-gather.2.cloned.1.call-done) | data formatting | bytes 8388608 | tf_op jit(solution)/shard_map/all_gather | solution.py:68
  659.6 6.0 reshape.179
  (22 shorter events, 0.5 us)
Async XLA Ops:
  7.2 4.4 copy-start.2
  7.2 109.8 %all-reduce.2.cloned.1.call-start = ((), (), s32[]{:S(2)}) async-start(), calls=%async_computation.2 | async-start | bytes 4194304 | tf_op jit(solution)/shard_map/psum | solution.py:12
  12.7 201.5 %all-to-all-start = ((s32[32,1,2]{2,1,0:T(1,128)}), s32[32,1,2]{2,1,0:T(1,128)S(1)}, u32[]{:S(2)}, u32[]{:S(2)}) async-start(s32[32,1,2]{2,1,0:T(1,128)} %bitcast.14), calls=%async_computation | async-start | bytes 32768 | tf_op jit(solution)/shard_map/all_to_all | solution.py:56
  20.0 9.5 %copy-start.1 = (s32[384,16]{0,1:T(8,128)S(1)}, s32[384,16]{0,1:T(8,128)}, u32[]{:S(2)}) copy-start(s32[384,16]{0,1:T(8,128)} %param.9) | copy-start | bytes 73732
  29.6 93.6 %copy-start = (f32[384,512]{1,0:T(8,128)S(1)}, f32[384,512]{1,0:T(8,128)}, u32[]{:S(2)}) copy-start(f32[384,512]{1,0:T(8,128)} %param.7) | copy-start | bytes 2359300
  214.2 379.5 %all-to-all-start.1 = ((f32[32,2,65536]{2,1,0:T(2,128)}), f32[32,2,65536]{2,1,0:T(2,128)}, u32[]{:S(2)}, u32[]{:S(2)}) async-start(f32[32,2,65536]{2,1,0:T(2,128)} %reshape.177), calls=%async_computation.1 | async-start | bytes 33554432 | tf_op jit(solution)/shard_map/all_to_all | solution.py:55
  218.7 434.1 %all-gather.2.cloned.1.call-start = ((), (), s32[]{:S(2)}) async-start(), calls=%async_computation.3 | async-start | bytes 5242880 | tf_op jit(solution)/shard_map/all_gather | solution.py:68
Sparse Core Ops, SparseCore 0:
  12.2 104.6 all-reduce.1
  622.0 30.7 all-gather.1
where the time goes:
time: 674 us; the launch traced here: 672 us
  waiting for transfers between devices  469 us (70%)
  local copies, waits for them, and re-layouts  94.7 us (14%)
  matrix products  77.4 us (11%)
  between operations  14.8 us (2%)
  starting transfers between devices  11.8 us (2%)
    all_to_all x1, waiting for transfers between devices, shards(): lax.all_to_all(sendbuf, ('work', 'serv'), split_axis=0, concat_axis=0, ti...  364 us
    psum x1, waiting for transfers between devices, broadcast(): return lax.psum(jnp.where(mine, value, jnp.zeros_like(value)), axis)  87.4 us
    dot_general x1, matrix products, shards(): jnp.einsum('sk,kwx->wsx', onehot, pieces, precision=lax.Precision.HIGHEST)  25.8 us
    reshape x1, local copies, waits for them, and re-layouts, shards(): pieces = item_grad.reshape(count, workers, piece * width)  20.5 us
    reshape x1, local copies, waits for them, and re-layouts, shards(): received.reshape(workers * servers * CAP, piece * width)  17.6 us
    all_gather x1, waiting for transfers between devices, shards(): whole = lax.all_gather(updated, 'work', axis=1, tiled=True)  17.5 us
    reshape x1, local copies, waits for them, and re-layouts, shards(): sendbuf = sendbuf.reshape(workers * servers, CAP, piece * width)  17.1 us
    dot_general x1, matrix products, shards(): jnp.einsum('ur,kbr->ukb', user_b, used, preferred_element_type=jnp.float32)  16.6 us
  transfers between devices with their start and end apart: 4, of which 3 were waited for; matrix products, arithmetic and copies ran while one was open for 20% of the time, Pallas kernels for 0%

commit v1 on v0

v1 whole, which is shorter than its diff:
```python
import functools

import jax
import jax.numpy as jnp
from jax import lax
from jax.experimental import pallas as pl
from jax.experimental.pallas import tpu as pltpu
from jax.sharding import PartitionSpec as P

BPS = 4
CAP = 2
CHUNKS = 2
GROUPS = ((8, "wsz"), (8, "swz"))


def tile_kernel(rows, tile_ref, fresh_ref, pick_ref, core_ref, user_ref, mark_ref, rate_ref, stale_ref, new_ref,
                keep_ref, send_ref, ugrad_ref, grad_ref):
    slot = pl.program_id(0)

    @pl.when(slot == 0)
    def _():
        ugrad_ref[...] = jnp.zeros_like(ugrad_ref)

    tile = tile_ref[slot]

    @pl.when(tile < 0)
    def _():
        keep_ref[...] = jnp.zeros_like(keep_ref)
        send_ref[...] = jnp.zeros_like(send_ref)

    @pl.when(tile >= 0)
    def _():
        user_b = user_ref[...].astype(jnp.bfloat16)
        take = jnp.full(stale_ref.shape[1:], fresh_ref[slot], jnp.int32) == 1
        used = jnp.where(take, new_ref[0], stale_ref[0])
        pred = lax.dot_general(user_b, used, (((1,), (1,)), ((), ())), preferred_element_type=jnp.float32)
        marks = mark_ref[...]
        column = lax.broadcasted_iota(jnp.int32, marks.shape, 1)
        mark = jnp.sum(jnp.where(column == tile, marks, 0), axis=1, keepdims=True).astype(jnp.float32)
        err = (mark * (rate_ref[...].astype(jnp.float32) - pred)).astype(jnp.bfloat16)
        grad_ref[...] = lax.dot_general(err, user_b, (((0,), (0,)), ((), ())), preferred_element_type=jnp.float32)
        ugrad_ref[...] += jnp.dot(err, used, preferred_element_type=jnp.float32)
        core = core_ref[0]
        half = rows // 2
        keep_ref[0] = grad_ref[pl.ds(core * half, half), :].astype(jnp.bfloat16)
        send_ref[0] = grad_ref[pl.ds((1 - core) * half, half), :].astype(jnp.bfloat16)


def tiles(chunk, rows, block, scalars, users, marks, ratings, stale, fresh):
    slots = scalars[0].shape[0]
    n_users, width = users.shape
    per = block // rows

    def at(ref, i):
        return jnp.maximum(ref[i], 0)

    grid = pltpu.PrefetchScalarGridSpec(
        num_scalar_prefetch=4,
        grid=(slots,),
        in_specs=[
            pl.BlockSpec((n_users, width), lambda i, t, f, p, c: (0, 0)),
            pl.BlockSpec(marks.shape, lambda i, t, f, p, c: (0, 0)),
            pl.BlockSpec((n_users, rows), lambda i, t, f, p, c: (0, at(t, i) * per + chunk)),
            pl.BlockSpec((1, rows, width), lambda i, t, f, p, c: (at(t, i), chunk, 0)),
            pl.BlockSpec((1, rows, width), lambda i, t, f, p, c: (at(p, i), 0, 0)),
        ],
        out_specs=[
            pl.BlockSpec((1, rows // 2, width), lambda i, t, f, p, c: (i, 0, 0)),
            pl.BlockSpec((1, rows // 2, width), lambda i, t, f, p, c: (i, 0, 0)),
            pl.BlockSpec((n_users, width), lambda i, t, f, p, c: (0, 0)),
        ],
        scratch_shapes=[pltpu.VMEM((rows, width), jnp.float32)],
    )
    half = jax.ShapeDtypeStruct((slots, rows // 2, width), jnp.bfloat16)
    flops = 6 * slots * n_users * rows * width
    moved = 2 * slots * rows * (3 * width + n_users)
    return pl.pallas_call(
        functools.partial(tile_kernel, rows),
        grid_spec=grid,
        out_shape=(half, half, jax.ShapeDtypeStruct((n_users, width), jnp.float32)),
        compiler_params=pltpu.CompilerParams(vmem_limit_bytes=24 * 2**20),
        cost_estimate=pl.CostEstimate(flops=flops, bytes_accessed=moved, transcendentals=0),
    )(*scalars, users, marks, ratings, stale, fresh)


def swap(value, axis, bit):
    size = lax.axis_size(axis)
    return lax.ppermute(value, axis, [(i, i ^ (1 << bit)) for i in range(size)])


def my_bit(axis, bit):
    return (lax.axis_index(axis) >> bit) & 1


def spread(ids, value):
    out = []
    for j in range(BPS):
        hit = (ids == j)[..., None, None]
        out.append(jnp.sum(jnp.where(hit, value.astype(jnp.float32), 0.0), axis=-3, dtype=jnp.float32))
    return jnp.stack(out, axis=-3)


def steps_of(order, work_bits, serv_bits):
    out = []
    for name in order:
        if name == "w":
            out += [("work", b) for b in range(1, work_bits)]
        elif name == "s":
            out += [("serv", b) for b in range(min(1, serv_bits))]
        elif name == "z":
            out += [("serv", b) for b in range(1, serv_bits)]
        else:
            out += [("serv", b) for b in range(serv_bits - 1, 0, -1)]
    return out


def reduce_group(steps, ids, other_ids, kept, got, serv_bits):
    left = list(range(serv_bits - 1, -1, -1))
    lead = (2,) * serv_bits
    first = True
    kept, got = (v.reshape(lead + v.shape[1:]) for v in (kept, got))
    ids, other_ids = (v.reshape(lead + v.shape[1:]) for v in (ids, other_ids))
    for axis, bit in steps:
        here = my_bit(axis, bit)

        def part(value, which, has_rows=True):
            if axis == "serv":
                return lax.dynamic_index_in_dim(value, which, left.index(bit), keepdims=False)
            if not has_rows:
                return value
            dim = value.ndim - 2
            size = value.shape[dim] // 2
            return lax.dynamic_slice_in_dim(value, which * size, size, dim)

        def total(which):
            if first:
                return spread(part(ids, which, False), part(kept, which)) + spread(
                    part(other_ids, which, False), part(got, which)
                )
            return part(kept, which) + part(got, which).astype(jnp.float32)

        sent = swap(total(1 - here).astype(jnp.bfloat16), axis, bit)
        kept = total(here)
        got = sent
        if axis == "serv":
            left.remove(bit)
        first = False
    return kept + got.astype(jnp.float32)


def shards(user_factors, ratings, row_mask, touched, stale_cache, item_factors, roster):
    servers = lax.axis_size("serv")
    workers = lax.axis_size("work")
    work_bits = workers.bit_length() - 1
    serv_bits = servers.bit_length() - 1
    count = touched.shape[1]
    width = item_factors.shape[1]
    block = ratings.shape[1] // count
    rows = block // CHUNKS
    ids = touched[0]
    owners = ids // BPS
    order = jnp.arange(count, dtype=jnp.int32)
    same = (owners[:, None] == owners[None, :]) & (order[None, :] < order[:, None])
    slot = owners * CAP + jnp.sum(same.astype(jnp.int32), axis=1)
    slots_all = jnp.arange(servers * CAP, dtype=jnp.int32)
    placing = slot[None, :] == slots_all[:, None]
    tile = jnp.sum(jnp.where(placing, order[None, :] + 1, 0), axis=1) - 1
    slot_ids = jnp.sum(jnp.where(placing, ids[None, :] + 1, 0), axis=1) - 1
    is_fresh = ((slots_all // CAP == roster[0]) & (tile >= 0)).astype(jnp.int32)
    local = jnp.where(tile >= 0, slot_ids % BPS, -1)
    pick = jnp.where(is_fresh == 1, local, 0)
    core = my_bit("work", 0).reshape(1).astype(jnp.int32)
    other = swap(local, "work", 0)
    local = local.reshape(servers, CAP)
    other = other.reshape(servers, CAP)
    stale = stale_cache.reshape(count, block, width)
    mine = lax.axis_index("serv") == roster[0]
    items = item_factors.reshape(BPS, block, width)
    user_grad = 0.0
    pieces = []
    for chunk in range(CHUNKS):
        own = items[:, chunk * rows : (chunk + 1) * rows].astype(jnp.bfloat16)
        fresh = lax.psum(jnp.where(mine, own, jnp.zeros_like(own)), "serv")
        kept, send, ugrad = tiles(
            chunk, rows, block, (tile, is_fresh, pick, core), user_factors, row_mask, ratings, stale, fresh
        )
        user_grad = user_grad + ugrad
        half = rows // 2
        start = 0
        sums = []
        for share, route in GROUPS:
            size = half * share // 16
            cut = lambda v: v[:, start : start + size].reshape(servers, CAP, size, width)
            got = swap(send[:, start : start + size], "work", 0).reshape(servers, CAP, size, width)
            sums.append(
                reduce_group(steps_of(route, work_bits, serv_bits), local, other, cut(kept), got, serv_bits)
            )
            start += size
        mine_sum = jnp.concatenate(sums, axis=1).astype(jnp.bfloat16)
        whole = lax.all_gather(mine_sum, "work", axis=0)
        start = 0
        parts = []
        for share, _ in GROUPS:
            size = half * share // 16 // (workers // 2)
            part = whole[:, :, start : start + size].reshape((2,) * work_bits + (BPS, size, width))
            dims = (work_bits,) + tuple(range(work_bits - 1, -1, -1)) + (work_bits + 1, work_bits + 2)
            parts.append(part.transpose(dims).reshape(BPS, 2, half * share // 16, width))
            start += size
        pieces.append(jnp.concatenate(parts, axis=2).reshape(BPS, rows, width))
    users_next = user_factors - 0.05 * (0.1 * user_factors - user_grad)
    grad_sum = jnp.concatenate(pieces, axis=1).astype(jnp.float32)
    items_next = (items - 0.01 * (grad_sum + 0.1 * items)).reshape(BPS * block, width)
    return (users_next, items_next)


def solution(mesh):
    both = P(("work", "serv"), None)
    in_specs = (both, both, both, both, both, P("serv", None), P("work"))
    return jax.shard_map(shards, mesh=mesh, in_specs=in_specs, out_specs=(both, P("serv", None)), check_vma=False)
```

time: 674 us -> 321 us (0.48)
  waiting for transfers between devices: 469 us -> 183 us
  matrix products: 77.4 us -> 0 us
  local copies, waits for them, and re-layouts: 94.7 us -> 22.6 us
  other arithmetic: 4.76 us -> 48.6 us
  Pallas kernels: 0 us -> 32.2 us
  starting transfers between devices: 11.8 us -> 18.7 us
    all_to_all x2 -> x0, waiting for transfers between devices: 364 us -> none  [the longest x1 364 us: shards(): lax.all_to_all(sendbuf, ('work', 'serv'), split_axis=0, concat_axis=0, ti...]
    dot_general x5 -> x0, matrix products: 77.4 us -> none  [the longest x1 25.8 us: shards(): jnp.einsum('sk,kwx->wsx', onehot, pieces, precision=lax.Precision.HIGHEST)]
    reshape x5 -> x0, local copies, waits for them, and re-layouts: 67.5 us -> none  [the longest x1 20.5 us: shards(): pieces = item_grad.reshape(count, workers, piece * width)]
    ppermute x0 -> x21, waiting for transfers between devices: none -> 66.9 us  [swap(): return lax.ppermute(value, axis, [(i, i ^ 1 << bit) for i in range(size)])]
    pallas_call x0 -> x2, Pallas kernels: none -> 32.2 us  [tiles(): pl.pallas_call(functools.partial(tile_kernel, rows), grid_spec=grid, out_...]
    convert_element_type x1 -> x16, other arithmetic: 0.01 us -> 18.6 us  [reduce_group(): sent = swap(total(1 - here).astype(jnp.bfloat16), axis, bit)]
    ppermute x0 -> x21, starting transfers between devices: none -> 18.4 us  [swap(): return lax.ppermute(value, axis, [(i, i ^ 1 << bit) for i in range(size)])]
    reduce_sum x1 -> x4, other arithmetic: 0.18 us -> 17.4 us  [the longest x3 17.2 us: spread(): jnp.sum(jnp.where(hit, value.astype(jnp.float32), 0.0), axis=-3, dtype=jn...]
  transfers between devices with their start and end apart: 4 -> 24, of which waited for: 3 -> 13; matrix products, arithmetic and copies ran while one was open for 20% -> 15% of each run, Pallas kernels for 0% -> 5%
where the time goes in v1:
time: 321 us; the launch traced here: 320 us
  waiting for transfers between devices  183 us (57%)
  other arithmetic  48.6 us (15%)
  Pallas kernels  32.2 us (10%)
  local copies, waits for them, and re-layouts  22.6 us (7%)
  starting transfers between devices  18.7 us (6%)
  between operations  15.2 us (5%)
    psum x1, waiting for transfers between devices, shards(): fresh = lax.psum(jnp.where(mine, own, jnp.zeros_like(own)), 'serv')  103 us
    ppermute x21, waiting for transfers between devices, swap(): return lax.ppermute(value, axis, [(i, i ^ 1 << bit) for i in range(size)])  66.9 us
    pallas_call x2, Pallas kernels, tiles(): pl.pallas_call(functools.partial(tile_kernel, rows), grid_spec=grid, out_...  32.2 us
    convert_element_type x16, other arithmetic, reduce_group(): sent = swap(total(1 - here).astype(jnp.bfloat16), axis, bit)  18.6 us
    ppermute x21, starting transfers between devices, swap(): return lax.ppermute(value, axis, [(i, i ^ 1 << bit) for i in range(size)])  18.4 us
    reduce_sum x3, other arithmetic, spread(): jnp.sum(jnp.where(hit, value.astype(jnp.float32), 0.0), axis=-3, dtype=jn...  17.2 us
    unnamed x69, local copies, waits for them, and re-layouts  14.4 us
    all_gather x2, waiting for transfers between devices, shards(): whole = lax.all_gather(mine_sum, 'work', axis=0)  13.1 us
  transfers between devices with their start and end apart: 24, of which 13 were waited for; matrix products, arithmetic and copies ran while one was open for 15% of the time, Pallas kernels for 5%

profile of v1, /device:TPU:0, one launch (start us, length us, event | category | flops | bytes accessed | tf_op | source)
XLA Modules:
  0.0 320.1 jit_solution(5782699648414148891)
XLA Ops:
  7.9 2.5 convert.34
  14.4 102.7 %all-reduce.3.cloned.1.call-done = (bf16[4,256,512]{2,1,0:T(8,128)(2,1)}, bf16[4,256,512]{2,1,0:T(8,128)(2,1)}) async-done(((bf16[4,256,512]{2,1,0:T(8,128)(2,1)}, bf16[4,256,512]{2,1,0:T(8,128)(2,1)}), (bf16[4,256,512]{2,1,0:T(8,128)(2,1)}, bf16[4,256,512]{2,1,0:T(8,128)(2,1)})) %all-reduce.3.cloned.1.call-update) | async-done | bytes 2097168 | tf_op jit(solution)/shard_map/psum | solution.py:183
  117.2 3.4 %copy-done.1 = bf16[8192,512]{1,0:T(8,128)(2,1)S(1)} copy-done((bf16[8192,512]{1,0:T(8,128)(2,1)S(1)}, bf16[8192,512]{1,0:T(8,128)(2,1)}, u32[]{:S(2)}) %copy-start.1) | copy-done | bytes 8388632
  120.5 2.8 copy-done.2
  124.5 16.1 %shard_map.86 = (bf16[16,128,512]{2,1,0:T(8,128)(2,1)S(1)}, bf16[16,128,512]{2,1,0:T(8,128)(2,1)S(1)}, f32[384,512]{1,0:T(8,128)S(1)}) custom-call(s32[16]{0:T(128)S(1)} %get-tuple-element.197.tile_ref, s32[16]{0:T(128)S(1)} %get-tuple-element.142.fresh_ref, s32[16]{0:T(128)S(1)} %get-tuple-element.140.pick_ref, s32[1]{0:T(128)} %bitcast.6.core_ref, ...), custom_call_target="tpu_custom_call" | custom-call | flops 4831838208 | bytes 15728640 | tf_op jit(solution)/shard_map/pallas_call | solution.py:77
  142.1 16.1 %shard_map.87 = (bf16[16,128,512]{2,1,0:T(8,128)(2,1)S(1)}, bf16[16,128,512]{2,1,0:T(8,128)(2,1)S(1)}, f32[384,512]{1,0:T(8,128)S(1)}) custom-call(s32[16]{0:T(128)S(1)} %get-tuple-element.197.tile_ref, s32[16]{0:T(128)S(1)} %get-tuple-element.142.fresh_ref, s32[16]{0:T(128)S(1)} %get-tuple-element.140.pick_ref, s32[1]{0:T(128)} %bitcast.6.core_ref, ...), custom_call_target="tpu_custom_call" | custom-call | flops 4831838208 | bytes 15728640 | tf_op jit(solution)/shard_map/pallas_call | solution.py:77
  159.8 3.9 %fusion.62 = (f32[2,2,64,512]{3,2,1,0:T(8,128)S(1)}, f32[2,2,64,512]{3,2,1,0:T(8,128)S(1)}, f32[2,2,64,512]{3,2,1,0:T(8,128)S(1)}, f32[2,2,64,512]{3,2,1,0:T(8,1...) fusion(pred[2,2,2]{2,1,0:T(4,128)(4,1)S(1)} %bitcast.506, ...), kind=kLoop, calls=%fused_computation.136 | loop fusion | flops 7340032 | bytes 10485832 | tf_op jit(solution)/shard_map/reduce_sum | solution.py:99
  163.9 4.0 %fusion.66 = (f32[2,2,64,512]{3,2,1,0:T(8,128)S(1)}, f32[2,2,64,512]{3,2,1,0:T(8,128)S(1)}, f32[2,2,64,512]{3,2,1,0:T(8,128)S(1)}, f32[2,2,64,512]{3,2,1,0:T(8,1...) fusion(pred[2,2,2]{2,1,0:T(4,128)(4,1)S(1)} %bitcast.504, ...), kind=kLoop, calls=%fused_computation.140 | loop fusion | flops 7340032 | bytes 10485832 | tf_op jit(solution)/shard_map/reduce_sum | solution.py:99
  172.2 9.4 %fusion.30 = (f32[2,2,2,32,512]{4,3,2,1,0:T(8,128)S(1)}, f32[2,2,2,32,512]{4,3,2,1,0:T(8,128)S(1)}, f32[2,2,2,32,512]{4,3,2,1,0:T(8,128)S(1)}, f32[2,2,2,32,512]...) fusion(pred[2,2,2,2]{3,2,1,0:T(4,128)(4,1)S(1)} %get-tuple-elem, ...), kind=kLoop, calls=%fused_computation.104 | loop fusion | flops 14680064 | bytes 20971656 | tf_op jit(solution)/shard_map/reduce_sum | solution.py:99
  189.4 6.3 %collective-permute-done.17 = bf16[2,2,4,64,512]{4,3,2,0,1:T(8,128)(2,1)} collective-permute-done((bf16[2,2,4,64,512]{4,3,2,0,1:T(8,128)(2,1)}, bf16[2,2,4,64,512]{4,3,2,0,1:T(8,128)(2,1)}, u32[]{:S(2)}, u32[]{:S(2)}) %collective-permute-start.17) | collective-permute-done | bytes 1048608 | tf_op jit(solution)/shard_map/ppermute | solution.py:88
  195.7 2.7 add_convert_fusion
  199.9 8.3 %collective-permute-done.12 = bf16[2,2,2,4,32,512]{5,4,2,1,0,3:T(8,128)(2,1)S(1)} collective-permute-done((bf16[2,2,2,4,32,512]{5,4,2,1,0,3:T(8,128)(2,1)S(1)}, bf16[2,2,2,4,32,512]{5,4,2,1,0,3:T(8,128)(2,1)S(1)}, u32[]{:S(2)}, u32[]{:S(2)}) %collective-permute-start.12) | collective-permute-done | bytes 1048608 | tf_op jit(solution)/shard_map/ppermute | solution.py:88
  216.3 24.7 %collective-permute-done.18 = bf16[2,2,4,32,512]{4,3,2,0,1:T(8,128)(2,1)} collective-permute-done((bf16[2,2,4,32,512]{4,3,2,0,1:T(8,128)(2,1)}, bf16[2,2,4,32,512]{4,3,2,0,1:T(8,128)(2,1)}, u32[]{:S(2)}, u32[]{:S(2)}) %collective-permute-start.18) | collective-permute-done | bytes 524320 | tf_op jit(solution)/shard_map/ppermute | solution.py:88
  245.6 2.3 add_convert_fusion.2
  249.4 2.1 collective-permute-done.19
  251.6 2.2 collective-permute-start.20
  253.8 2.7 fusion.70
  259.2 6.2 %collective-permute-done.15 = bf16[4,32,512]{2,1,0:T(8,128)(2,1)S(1)} collective-permute-done((bf16[4,32,512]{2,1,0:T(8,128)(2,1)S(1)}, bf16[4,32,512]{2,1,0:T(8,128)(2,1)S(1)}, u32[]{:S(2)}, u32[]{:S(2)}) %collective-permute-start.15) | collective-permute-done | bytes 131104 | tf_op jit(solution)/shard_map/ppermute | solution.py:88
  269.1 2.1 collective-permute-start.4
  271.2 5.9 %collective-permute-done.9 = bf16[2,4,32,512]{3,2,1,0:T(8,128)(2,1)S(1)} collective-permute-done((bf16[2,4,32,512]{3,2,1,0:T(8,128)(2,1)S(1)}, bf16[2,4,32,512]{3,2,1,0:T(8,128)(2,1)S(1)}, u32[]{:S(2)}, u32[]{:S(2)}) %collective-permute-start.9) | collective-permute-done | bytes 262176 | tf_op jit(solution)/shard_map/ppermute | solution.py:88
  277.6 5.5 %collective-permute-done.4 = bf16[2,4,32,512]{3,2,0,1:T(8,128)(2,1)S(1)} collective-permute-done((bf16[2,4,32,512]{3,2,0,1:T(8,128)(2,1)S(1)}, bf16[2,4,32,512]{3,2,0,1:T(8,128)(2,1)S(1)}, u32[]{:S(2)}, u32[]{:S(2)}) %collective-permute-start.4) | collective-permute-done | bytes 262176 | tf_op jit(solution)/shard_map/ppermute | solution.py:88
  283.2 5.2 %collective-permute-done.10 = bf16[4,32,512]{2,1,0:T(8,128)(2,1)S(1)} collective-permute-done((bf16[4,32,512]{2,1,0:T(8,128)(2,1)S(1)}, bf16[4,32,512]{2,1,0:T(8,128)(2,1)S(1)}, u32[]{:S(2)}, u32[]{:S(2)}) %collective-permute-start.10) | collective-permute-done | bytes 131104 | tf_op jit(solution)/shard_map/ppermute | solution.py:88
  293.7 13.1 %all-gather.3.cloned.1.call-done = bf16[4,4,64,512]{3,2,1,0:T(8,128)(2,1)} async-done(((bf16[1,4,64,512]{3,2,1,0:T(8,128)(2,1)}), bf16[4,4,64,512]{3,2,1,0:T(8,128)(2,1)}) %all-gather.3.cloned.1.call-update) | async-done | bytes 1048592 | tf_op jit(solution)/shard_map/all_gather | solution.py:200
  310.6 3.0 fusion.1
  (191 shorter events, 51.6 us)
Async XLA Ops:
  7.2 110.0 %all-reduce.3.cloned.1.call-start = ((), (), s32[]{:S(2)}) async-start(), calls=%async_computation.2 | async-start | bytes 4194304 | tf_op jit(solution)/shard_map/psum | solution.py:183
  11.8 280.5 %all-gather.5.cloned.1.call-start = ((), (), s32[]{:S(2)}) async-start(), calls=%async_computation.1 | async-start | bytes 1310720 | tf_op jit(solution)/shard_map/all_gather | solution.py:200
  12.8 1.3 collective-permute-start
  141.8 22.0 %collective-permute-start.6 = (bf16[16,64,512]{2,1,0:T(8,128)(2,1)S(1)}, bf16[16,64,512]{2,1,0:T(8,128)(2,1)S(1)}, u32[]{:S(2)}, u32[]{:S(2)}) collective-permute-start(bf16[16,64,512]{2,1,0:T(8,128)(2,1)S(1)} %get-tuple-element.152), channel_id=1, source_target_pairs={{0,8},{8,0},{16,24},{24,16},{1,9},{9,1},{17,25},{25,17},{2,10},{10... | collective-permute-start | bytes 3145736 | tf_op jit(solution)/shard_map/ppermute | solution.py:88
  158.4 5.4 %collective-permute-start.16 = (bf16[16,64,512]{2,1,0:T(8,128)(2,1)S(1)}, bf16[16,64,512]{2,1,0:T(8,128)(2,1)S(1)}, u32[]{:S(2)}, u32[]{:S(2)}) collective-permute-start(bf16[16,64,512]{2,1,0:T(8,128)(2,1)S(1)} %get-tuple-element.154), channel_id=1, source_target_pairs={{0,8},{8,0},{16,24},{24,16},{1,9},{9,1},{17,25},{25,17},{2,10},{10... | collective-permute-start | bytes 3145736 | tf_op jit(solution)/shard_map/ppermute | solution.py:88
  158.8 12.1 %collective-permute-start.1 = (bf16[16,64,512]{2,1,0:T(8,128)(2,1)}, bf16[16,64,512]{2,1,0:T(8,128)(2,1)S(1)}, u32[]{:S(2)}, u32[]{:S(2)}) collective-permute-start(bf16[16,64,512]{2,1,0:T(8,128)(2,1)} %get-tuple-element.151), channel_id=1, source_target_pairs={{0,8},{8,0},{16,24},{24,16},{1,9},{9,1},{17,25},{25,17},{2,10},{10... | collective-permute-start | bytes 3145736 | tf_op jit(solution)/shard_map/ppermute | solution.py:88
  159.1 11.7 %collective-permute-start.11 = (bf16[16,64,512]{2,1,0:T(8,128)(2,1)S(1)}, bf16[16,64,512]{2,1,0:T(8,128)(2,1)S(1)}, u32[]{:S(2)}, u32[]{:S(2)}) collective-permute-start(bf16[16,64,512]{2,1,0:T(8,128)(2,1)S(1)} %get-tuple-element.153), channel_id=1, source_target_pairs={{0,8},{8,0},{16,24},{24,16},{1,9},{9,1},{17,25},{25,17},{2,10},{10... | collective-permute-start | bytes 3145736 | tf_op jit(solution)/shard_map/ppermute | solution.py:88
  169.4 26.3 %collective-permute-start.17 = (bf16[2,2,4,64,512]{4,3,2,0,1:T(8,128)(2,1)}, bf16[2,2,4,64,512]{4,3,2,0,1:T(8,128)(2,1)}, u32[]{:S(2)}, u32[]{:S(2)}) collective-permute-start(bf16[2,2,4,64,512]{4,3,2,0,1:T(8,128)(2,1)} %fusion.5), channel_id=1, source_target_pairs={{0,1},{1,0},{2,3},{3,2},{4,5},{5,4},{6,7},{7,6},{8,9},{9,8},{10,11... | collective-permute-start | bytes 3145736 | tf_op jit(solution)/shard_map/ppermute | solution.py:88
  182.1 26.1 %collective-permute-start.12 = (bf16[2,2,2,4,32,512]{5,4,2,1,0,3:T(8,128)(2,1)S(1)}, bf16[2,2,2,4,32,512]{5,4,2,1,0,3:T(8,128)(2,1)S(1)}, u32[]{:S(2)}, u32[]{:S(2)}) collective-permute-start(bf16[2,2,2,4,32,512]{5,4,2,1,0,3:T(8,128)(2,1)S(1)} %fusion.4), channel_id=1, source_target_pairs={{0,16},{8,24},{16,0},{24,8},{1,17},{9,25},{17,1},{25,9},{2,18},{10... | collective-permute-start | bytes 3145736 | tf_op jit(solution)/shard_map/ppermute | solution.py:88
  185.7 59.9 %collective-permute-start.7 = (bf16[2,2,4,64,512]{4,3,2,0,1:T(8,128)(2,1)}, bf16[2,2,4,64,512]{4,3,2,0,1:T(8,128)(2,1)}, u32[]{:S(2)}, u32[]{:S(2)}) collective-permute-start(bf16[2,2,4,64,512]{4,3,2,0,1:T(8,128)(2,1)} %fusion.3), channel_id=1, source_target_pairs={{0,1},{1,0},{2,3},{3,2},{4,5},{5,4},{6,7},{7,6},{8,9},{9,8},{10,11... | collective-permute-start | bytes 3145736 | tf_op jit(solution)/shard_map/ppermute | solution.py:88
  187.6 66.2 %collective-permute-start.2 = (bf16[2,2,2,4,32,512]{5,4,2,1,0,3:T(8,128)(2,1)}, bf16[2,2,2,4,32,512]{5,4,2,1,0,3:T(8,128)(2,1)}, u32[]{:S(2)}, u32[]{:S(2)}) collective-permute-start(bf16[2,2,2,4,32,512]{5,4,2,1,0,3:T(8,128)(2,1)} %fusion.2), channel_id=1, source_target_pairs={{0,16},{8,24},{16,0},{24,8},{1,17},{9,25},{17,1},{25,9},{2,18},{10... | collective-permute-start | bytes 3145736 | tf_op jit(solution)/shard_map/ppermute | solution.py:88
  198.4 42.6 %collective-permute-start.18 = (bf16[2,2,4,32,512]{4,3,2,0,1:T(8,128)(2,1)}, bf16[2,2,4,32,512]{4,3,2,0,1:T(8,128)(2,1)}, u32[]{:S(2)}, u32[]{:S(2)}) collective-permute-start(bf16[2,2,4,32,512]{4,3,2,0,1:T(8,128)(2,1)} %get-tuple-element.149), channel_id=1, source_target_pairs={{0,16},{8,24},{16,0},{24,8},{1,17},{9,25},{17,1},{25,9},{2,18},{10... | collective-permute-start | bytes 1572872 | tf_op jit(solution)/shard_map/ppermute | solution.py:88
  209.4 34.4 %collective-permute-start.13 = (bf16[2,2,4,32,512]{4,3,1,0,2:T(8,128)(2,1)}, bf16[2,2,4,32,512]{4,3,1,0,2:T(8,128)(2,1)}, u32[]{:S(2)}, u32[]{:S(2)}) collective-permute-start(bf16[2,2,4,32,512]{4,3,1,0,2:T(8,128)(2,1)} %get-tuple-element.147), channel_id=1, source_target_pairs={{0,1},{1,0},{2,3},{3,2},{4,5},{5,4},{6,7},{7,6},{8,9},{9,8},{10,11... | collective-permute-start | bytes 1572872 | tf_op jit(solution)/shard_map/ppermute | solution.py:88
  242.2 9.3 %collective-permute-start.19 = (bf16[2,4,32,512]{3,2,1,0:T(8,128)(2,1)S(1)}, bf16[2,4,32,512]{3,2,1,0:T(8,128)(2,1)S(1)}, u32[]{:S(2)}, u32[]{:S(2)}) collective-permute-start(bf16[2,4,32,512]{3,2,1,0:T(8,128)(2,1)S(1)} %get-tuple-element.167), channel_id=1, source_target_pairs={{0,2},{1,3},{2,0},{3,1},{4,6},{5,7},{6,4},{7,5},{8,10},{9,11},{10,... | collective-permute-start | bytes 786440 | tf_op jit(solution)/shard_map/ppermute | solution.py:88
  244.9 12.3 %collective-permute-start.14 = (bf16[2,4,32,512]{3,2,0,1:T(8,128)(2,1)S(1)}, bf16[2,4,32,512]{3,2,0,1:T(8,128)(2,1)S(1)}, u32[]{:S(2)}, u32[]{:S(2)}) collective-permute-start(bf16[2,4,32,512]{3,2,0,1:T(8,128)(2,1)S(1)} %get-tuple-element.165), channel_id=1, source_target_pairs={{0,2},{1,3},{2,0},{3,1},{4,6},{5,7},{6,4},{7,5},{8,10},{9,11},{10,... | collective-permute-start | bytes 786440 | tf_op jit(solution)/shard_map/ppermute | solution.py:88
  248.0 18.5 %collective-permute-start.8 = (bf16[2,2,4,32,512]{4,3,2,0,1:T(8,128)(2,1)}, bf16[2,2,4,32,512]{4,3,2,0,1:T(8,128)(2,1)}, u32[]{:S(2)}, u32[]{:S(2)}) collective-permute-start(bf16[2,2,4,32,512]{4,3,2,0,1:T(8,128)(2,1)} %get-tuple-element.145), channel_id=1, source_target_pairs={{0,16},{8,24},{16,0},{24,8},{1,17},{9,25},{17,1},{25,9},{2,18},{10... | collective-permute-start | bytes 1572872 | tf_op jit(solution)/shard_map/ppermute | solution.py:88
  251.6 7.5 %collective-permute-start.20 = (bf16[4,32,512]{2,1,0:T(8,128)(2,1)S(1)}, bf16[4,32,512]{2,1,0:T(8,128)(2,1)S(1)}, u32[]{:S(2)}, u32[]{:S(2)}) collective-permute-start(bf16[4,32,512]{2,1,0:T(8,128)(2,1)S(1)} %fusion.93), channel_id=1, source_target_pairs={{0,4},{1,5},{2,6},{3,7},{4,0},{5,1},{6,2},{7,3},{8,12},{9,13},{10,... | collective-permute-start | bytes 393224 | tf_op jit(solution)/shard_map/ppermute | solution.py:88
  256.5 11.3 %collective-permute-start.3 = (bf16[2,2,4,32,512]{4,3,1,0,2:T(8,128)(2,1)}, bf16[2,2,4,32,512]{4,3,1,0,2:T(8,128)(2,1)}, u32[]{:S(2)}, u32[]{:S(2)}) collective-permute-start(bf16[2,2,4,32,512]{4,3,1,0,2:T(8,128)(2,1)} %get-tuple-element.143), channel_id=1, source_target_pairs={{0,1},{1,0},{2,3},{3,2},{4,5},{5,4},{6,7},{7,6},{8,9},{9,8},{10,11... | collective-permute-start | bytes 1572872 | tf_op jit(solution)/shard_map/ppermute | solution.py:88
  257.3 8.1 %collective-permute-start.15 = (bf16[4,32,512]{2,1,0:T(8,128)(2,1)S(1)}, bf16[4,32,512]{2,1,0:T(8,128)(2,1)S(1)}, u32[]{:S(2)}, u32[]{:S(2)}) collective-permute-start(bf16[4,32,512]{2,1,0:T(8,128)(2,1)S(1)} %fusion.91), channel_id=1, source_target_pairs={{0,4},{1,5},{2,6},{3,7},{4,0},{5,1},{6,2},{7,3},{8,12},{9,13},{10,... | collective-permute-start | bytes 393224 | tf_op jit(solution)/shard_map/ppermute | solution.py:88
  266.2 40.7 %all-gather.3.cloned.1.call-start = ((), (), s32[]{:S(2)}) async-start(), calls=%async_computation | async-start | bytes 1310720 | tf_op jit(solution)/shard_map/all_gather | solution.py:200
  267.8 9.3 %collective-permute-start.9 = (bf16[2,4,32,512]{3,2,1,0:T(8,128)(2,1)S(1)}, bf16[2,4,32,512]{3,2,1,0:T(8,128)(2,1)S(1)}, u32[]{:S(2)}, u32[]{:S(2)}) collective-permute-start(bf16[2,4,32,512]{3,2,1,0:T(8,128)(2,1)S(1)} %get-tuple-element.163), channel_id=1, source_target_pairs={{0,2},{1,3},{2,0},{3,1},{4,6},{5,7},{6,4},{7,5},{8,10},{9,11},{10,... | collective-permute-start | bytes 786440 | tf_op jit(solution)/shard_map/ppermute | solution.py:88
  269.1 13.9 %collective-permute-start.4 = (bf16[2,4,32,512]{3,2,0,1:T(8,128)(2,1)S(1)}, bf16[2,4,32,512]{3,2,0,1:T(8,128)(2,1)S(1)}, u32[]{:S(2)}, u32[]{:S(2)}) collective-permute-start(bf16[2,4,32,512]{3,2,0,1:T(8,128)(2,1)S(1)} %get-tuple-element.161), channel_id=1, source_target_pairs={{0,2},{1,3},{2,0},{3,1},{4,6},{5,7},{6,4},{7,5},{8,10},{9,11},{10,... | collective-permute-start | bytes 786440 | tf_op jit(solution)/shard_map/ppermute | solution.py:88
  277.1 11.2 %collective-permute-start.10 = (bf16[4,32,512]{2,1,0:T(8,128)(2,1)S(1)}, bf16[4,32,512]{2,1,0:T(8,128)(2,1)S(1)}, u32[]{:S(2)}, u32[]{:S(2)}) collective-permute-start(bf16[4,32,512]{2,1,0:T(8,128)(2,1)S(1)} %fusion.89), channel_id=1, source_target_pairs={{0,4},{1,5},{2,6},{3,7},{4,0},{5,1},{6,2},{7,3},{8,12},{9,13},{10,... | collective-permute-start | bytes 393224 | tf_op jit(solution)/shard_map/ppermute | solution.py:88
  283.1 7.3 %collective-permute-start.5 = (bf16[4,32,512]{2,1,0:T(8,128)(2,1)S(1)}, bf16[4,32,512]{2,1,0:T(8,128)(2,1)S(1)}, u32[]{:S(2)}, u32[]{:S(2)}) collective-permute-start(bf16[4,32,512]{2,1,0:T(8,128)(2,1)S(1)} %fusion.87), channel_id=1, source_target_pairs={{0,4},{1,5},{2,6},{3,7},{4,0},{5,1},{6,2},{7,3},{8,12},{9,13},{10,... | collective-permute-start | bytes 393224 | tf_op jit(solution)/shard_map/ppermute | solution.py:88
  (26 other events, 171.2 us)
Sparse Core Ops, SparseCore 0:
  12.2 104.8 all-reduce.2
  266.3 15.2 all-gather.4
  291.3 15.5 all-gather.2

commit v2 on v1

v2 whole, which is shorter than its diff:
```python
import functools

import jax
import jax.numpy as jnp
from jax import lax
from jax.experimental import pallas as pl
from jax.experimental.pallas import tpu as pltpu
from jax.sharding import PartitionSpec as P

BPS = 4
CAP = 2
GROUPS = ((4, "wsz"), (4, "swz"), (4, "wsz"), (4, "swz"))
CAST_ROUTES = ("sz", "zs")
TILES_PER_CALL = 3


def tile_kernel(rows, slot_ref, tile_ref, source_ref, core_ref, user_ref, mark_ref, rate_ref, used_ref, before_ref,
                keep_in, send_in, keep_ref, send_ref, ugrad_ref, grad_ref):
    step = pl.program_id(0)

    @pl.when(step == 0)
    def _():
        ugrad_ref[...] = before_ref[...]

    tile = tile_ref[step]

    @pl.when(tile < 0)
    def _():
        keep_ref[...] = jnp.zeros_like(keep_ref)
        send_ref[...] = jnp.zeros_like(send_ref)

    @pl.when(tile >= 0)
    def _():
        user_b = user_ref[...].astype(jnp.bfloat16)
        used = used_ref[0]
        pred = lax.dot_general(user_b, used, (((1,), (1,)), ((), ())), preferred_element_type=jnp.float32)
        marks = mark_ref[...]
        column = lax.broadcasted_iota(jnp.int32, marks.shape, 1)
        mark = jnp.sum(jnp.where(column == tile, marks, 0), axis=1, keepdims=True).astype(jnp.float32)
        err = (mark * (rate_ref[...].astype(jnp.float32) - pred)).astype(jnp.bfloat16)
        grad_ref[...] = lax.dot_general(err, user_b, (((0,), (0,)), ((), ())), preferred_element_type=jnp.float32)
        ugrad_ref[...] += jnp.dot(err, used, preferred_element_type=jnp.float32)
        core = core_ref[0]
        half = rows // 2
        keep_ref[0] = grad_ref[pl.ds(core * half, half), :].astype(jnp.bfloat16)
        send_ref[0] = grad_ref[pl.ds((1 - core) * half, half), :].astype(jnp.bfloat16)


def tiles(scalars, users, marks, ratings, source, ugrad, keep, send):
    n = scalars[0].shape[0]
    n_users, width = users.shape
    rows = source.shape[1]

    def at(ref, i):
        return jnp.maximum(ref[i], 0)

    out_block = pl.BlockSpec((1, rows // 2, width), lambda i, s, t, f, c: (s[i], 0, 0))
    whole = pl.BlockSpec((n_users, width), lambda i, s, t, f, c: (0, 0))
    grid = pltpu.PrefetchScalarGridSpec(
        num_scalar_prefetch=4,
        grid=(n,),
        in_specs=[
            whole,
            pl.BlockSpec(marks.shape, lambda i, s, t, f, c: (0, 0)),
            pl.BlockSpec((n_users, rows), lambda i, s, t, f, c: (0, at(t, i))),
            pl.BlockSpec((1, rows, width), lambda i, s, t, f, c: (at(f, i), 0, 0)),
            whole,
            pl.BlockSpec(memory_space=pl.ANY),
            pl.BlockSpec(memory_space=pl.ANY),
        ],
        out_specs=[out_block, out_block, whole],
        scratch_shapes=[pltpu.VMEM((rows, width), jnp.float32)],
    )
    half = jax.ShapeDtypeStruct(keep.shape, jnp.bfloat16)
    flops = 6 * n * n_users * rows * width
    moved = 2 * n * rows * (3 * width + n_users) + 12 * n_users * width
    return pl.pallas_call(
        functools.partial(tile_kernel, rows),
        grid_spec=grid,
        out_shape=(half, half, jax.ShapeDtypeStruct((n_users, width), jnp.float32)),
        input_output_aliases={9: 0, 10: 1},
        compiler_params=pltpu.CompilerParams(vmem_limit_bytes=56 * 2**20),
        cost_estimate=pl.CostEstimate(flops=flops, bytes_accessed=moved, transcendentals=0),
    )(*scalars, users, marks, ratings, source, ugrad, keep, send)


def swap(value, axis, bit):
    size = lax.axis_size(axis)
    return lax.ppermute(value, axis, [(i, i ^ (1 << bit)) for i in range(size)])


def my_bit(axis, bit):
    return (lax.axis_index(axis) >> bit) & 1


def spread(ids, value):
    out = []
    for j in range(BPS):
        hit = (ids == j)[..., None, None]
        out.append(jnp.sum(jnp.where(hit, value.astype(jnp.float32), 0.0), axis=-3, dtype=jnp.float32))
    return jnp.stack(out, axis=-3)


def steps_of(order, work_bits, serv_bits):
    out = []
    for name in order:
        if name == "w":
            out += [("work", b) for b in range(1, work_bits)]
        elif name == "s":
            out += [("serv", b) for b in range(min(1, serv_bits))]
        elif name == "z":
            out += [("serv", b) for b in range(1, serv_bits)]
        else:
            out += [("serv", b) for b in range(serv_bits - 1, 0, -1)]
    return out


def reduce_group(steps, ids, other_ids, kept, got, serv_bits):
    left = list(range(serv_bits - 1, -1, -1))
    lead = (2,) * serv_bits
    first = True
    kept, got = (v.reshape(lead + v.shape[1:]) for v in (kept, got))
    ids, other_ids = (v.reshape(lead + v.shape[1:]) for v in (ids, other_ids))
    for axis, bit in steps:
        here = my_bit(axis, bit)

        def part(value, which, has_rows=True):
            if axis == "serv":
                return lax.dynamic_index_in_dim(value, which, left.index(bit), keepdims=False)
            if not has_rows:
                return value
            dim = value.ndim - 2
            size = value.shape[dim] // 2
            return lax.dynamic_slice_in_dim(value, which * size, size, dim)

        def total(which):
            if first:
                return spread(part(ids, which, False), part(kept, which)) + spread(
                    part(other_ids, which, False), part(got, which)
                )
            return part(kept, which) + part(got, which).astype(jnp.float32)

        sent = swap(total(1 - here).astype(jnp.bfloat16), axis, bit)
        kept = total(here)
        got = sent
        if axis == "serv":
            left.remove(bit)
        first = False
    return kept + got.astype(jnp.float32)


def cast_step(root, value, bits, step):
    if step < len(bits):
        bit = bits[step]
        here = my_bit("serv", bit)
        size = value.shape[1] // 2
        got = swap(lax.dynamic_slice_in_dim(value, (1 - here) * size, size, 1), "serv", bit)
        own = lax.dynamic_slice_in_dim(value, here * size, size, 1)
        return jnp.where(((root >> bit) & 1) == here, own, got)
    bit = bits[2 * len(bits) - 1 - step]
    low = my_bit("serv", bit) == 0
    got = swap(value, "serv", bit)
    return jnp.concatenate([jnp.where(low, value, got), jnp.where(low, got, value)], axis=1)


def shards(user_factors, ratings, row_mask, touched, stale_cache, item_factors, roster):
    servers = lax.axis_size("serv")
    workers = lax.axis_size("work")
    work_bits = workers.bit_length() - 1
    serv_bits = servers.bit_length() - 1
    count = touched.shape[1]
    width = item_factors.shape[1]
    block = ratings.shape[1] // count
    ids = touched[0]
    owners = ids // BPS
    order = jnp.arange(count, dtype=jnp.int32)
    same = (owners[:, None] == owners[None, :]) & (order[None, :] < order[:, None])
    slot = owners * CAP + jnp.sum(same.astype(jnp.int32), axis=1)
    slots_all = jnp.arange(servers * CAP, dtype=jnp.int32)
    placing = slot[None, :] == slots_all[:, None]
    tile = jnp.sum(jnp.where(placing, order[None, :] + 1, 0), axis=1) - 1
    slot_ids = jnp.sum(jnp.where(placing, ids[None, :] + 1, 0), axis=1) - 1
    local = jnp.where(tile >= 0, slot_ids % BPS, -1)
    core = my_bit("work", 0).reshape(1).astype(jnp.int32)
    other = swap(local, "work", 0).reshape(servers, CAP)
    root = roster[0]
    stale = stale_cache.reshape(count, block, width)
    items = item_factors.reshape(BPS, block, width)
    items_b = items.astype(jnp.bfloat16)
    share = block // len(CAST_ROUTES)
    cast = [items_b[:, i * share : (i + 1) * share] for i in range(len(CAST_ROUTES))]
    bits = [[b for _, b in steps_of(r, work_bits, serv_bits)] for r in CAST_ROUTES]
    kept = jnp.zeros((servers * CAP, block // 2, width), jnp.bfloat16)
    send = jnp.zeros_like(kept)
    user_grad = jnp.zeros(user_factors.shape, jnp.float32)
    rest = (servers - 1) * CAP
    starts = list(range(0, rest, TILES_PER_CALL))
    for step in range(max(2 * serv_bits, len(starts))):
        if step < 2 * serv_bits:
            cast = [cast_step(root, v, b, step) for v, b in zip(cast, bits)]
        if step < len(starts):
            start = starts[step]
            places = jnp.arange(start, min(start + TILES_PER_CALL, rest), dtype=jnp.int32)
            places = places + jnp.where(places >= root * CAP, CAP, 0)
            these = jnp.take(tile, places)
            kept, send, user_grad = tiles(
                (places, these, these, core), user_factors, row_mask, ratings, stale, user_grad, kept, send
            )
            cast, user_grad = lax.optimization_barrier((cast, user_grad))
    fresh = jnp.concatenate(cast, axis=1)
    places = root * CAP + jnp.arange(CAP, dtype=jnp.int32)
    scalars = (places, jnp.take(tile, places), jnp.take(local, places), core)
    kept, send, user_grad = tiles(scalars, user_factors, row_mask, ratings, fresh, user_grad, kept, send)
    local = local.reshape(servers, CAP)
    half = block // 2
    start = 0
    sums = []
    for part, route in GROUPS:
        size = half * part // 16
        got = swap(send[:, start : start + size], "work", 0).reshape(servers, CAP, size, width)
        mine = kept[:, start : start + size].reshape(servers, CAP, size, width)
        sums.append(reduce_group(steps_of(route, work_bits, serv_bits), local, other, mine, got, serv_bits))
        start += size
    mine_sum = jnp.concatenate(sums, axis=1).astype(jnp.bfloat16)
    whole = lax.all_gather(mine_sum, "work", axis=0)
    start = 0
    parts = []
    for part, _ in GROUPS:
        size = half * part // 16 // (workers // 2)
        piece = whole[:, :, start : start + size].reshape((2,) * work_bits + (BPS, size, width))
        dims = (work_bits,) + tuple(range(work_bits - 1, -1, -1)) + (work_bits + 1, work_bits + 2)
        parts.append(piece.transpose(dims).reshape(BPS, 2, half * part // 16, width))
        start += size
    grad_sum = jnp.concatenate(parts, axis=2).reshape(BPS, block, width).astype(jnp.float32)
    users_next = user_factors - 0.05 * (0.1 * user_factors - user_grad)
    items_next = (items - 0.01 * (grad_sum + 0.1 * items)).reshape(BPS * block, width)
    return (users_next, items_next)


def solution(mesh):
    both = P(("work", "serv"), None)
    in_specs = (both, both, both, both, both, P("serv", None), P("work"))
    return jax.shard_map(shards, mesh=mesh, in_specs=in_specs, out_specs=(both, P("serv", None)), check_vma=False)
```

time: 321 us -> 270 us (0.84)
  waiting for transfers between devices: 183 us -> 114 us
  starting transfers between devices: 18.7 us -> 35.6 us
  Pallas kernels: 32.2 us -> 39.8 us
  other arithmetic: 48.6 us -> 42.2 us
    psum x1 -> x0, waiting for transfers between devices: 103 us -> none  [shards(): fresh = lax.psum(jnp.where(mine, own, jnp.zeros_like(own)), 'serv')]
    ppermute x21 -> x33, waiting for transfers between devices: 66.9 us -> 93.8 us  [swap(): return lax.ppermute(value, axis, [(i, i ^ 1 << bit) for i in range(size)])]
    ppermute x21 -> x33, starting transfers between devices: 18.4 us -> 35.6 us  [swap(): return lax.ppermute(value, axis, [(i, i ^ 1 << bit) for i in range(size)])]
    unnamed x69 -> x29, local copies, waits for them, and re-layouts: 14.4 us -> 2.97 us
    pallas_call x2 -> x6, Pallas kernels: 32.2 us -> 39.8 us  [tiles(): pl.pallas_call(functools.partial(tile_kernel, rows), grid_spec=grid, out_...]
    all_gather x2 -> x1, waiting for transfers between devices: 13.1 us -> 19.9 us  [shards(): whole = lax.all_gather(mine_sum, 'work', axis=0)]
    convert_element_type x16, other arithmetic: 18.6 us -> 12.4 us  [reduce_group(): sent = swap(total(1 - here).astype(jnp.bfloat16), axis, bit)]
    reduce_sum x3 -> x4, other arithmetic: 17.2 us -> 11.2 us  [spread(): jnp.sum(jnp.where(hit, value.astype(jnp.float32), 0.0), axis=-3, dtype=jn...]
  transfers between devices with their start and end apart: 24 -> 34, of which waited for: 13 -> 17; matrix products, arithmetic and copies ran while one was open for 15% -> 18% of each run, Pallas kernels for 5% -> 13%
where the time goes in v2:
time: 270 us; the launch traced here: 269 us
  waiting for transfers between devices  114 us (42%)
  other arithmetic  42.2 us (16%)
  Pallas kernels  39.8 us (15%)
  starting transfers between devices  35.6 us (13%)
  local copies, waits for them, and re-layouts  21.5 us (8%)
  between operations  15.8 us (6%)
    ppermute x33, waiting for transfers between devices, swap(): return lax.ppermute(value, axis, [(i, i ^ 1 << bit) for i in range(size)])  93.8 us
    pallas_call x6, Pallas kernels, tiles(): pl.pallas_call(functools.partial(tile_kernel, rows), grid_spec=grid, out_...  39.8 us
    ppermute x33, starting transfers between devices, swap(): return lax.ppermute(value, axis, [(i, i ^ 1 << bit) for i in range(size)])  35.6 us
    all_gather x1, waiting for transfers between devices, shards(): whole = lax.all_gather(mine_sum, 'work', axis=0)  19.9 us
    convert_element_type x16, other arithmetic, reduce_group(): sent = swap(total(1 - here).astype(jnp.bfloat16), axis, bit)  12.4 us
    reduce_sum x4, other arithmetic, spread(): jnp.sum(jnp.where(hit, value.astype(jnp.float32), 0.0), axis=-3, dtype=jn...  11.2 us
  transfers between devices with their start and end apart: 34, of which 17 were waited for; matrix products, arithmetic and copies ran while one was open for 18% of the time, Pallas kernels for 13%

profile of v2, /device:TPU:0, one launch (start us, length us, event | category | flops | bytes accessed | tf_op | source)
XLA Modules:
  0.0 268.7 jit_solution(10912221010835688003)
XLA Ops:
  9.9 3.0 %collective-permute-start = (bf16[4,128,512]{2,1,0:T(8,128)(2,1)S(1)}, bf16[4,128,512]{2,1,0:T(8,128)(2,1)}, u32[]{:S(2)}, u32[]{:S(2)}) collective-permute-start(bf16[4,128,512]{2,1,0:T(8,128)(2,1)S(1)} %constant_dynamic-slice_fusion.9), channel_id=1, source_target_pairs={{0,1},{1,0},{2,3},{3,2},{4,5},{5,4},{6,7},{7,6},{8,9},{9,8},{10,11... | collective-permute-start | bytes 1572872 | tf_op jit(solution)/shard_map/ppermute | solution.py:89
  29.2 7.1 %shard_map.86 = (bf16[16,256,512]{2,1,0:T(8,128)(2,1)}, bf16[16,256,512]{2,1,0:T(8,128)(2,1)}, f32[384,512]{1,0:T(8,128)}) custom-call(s32[3]{0:T(128)} %get-tuple-element.273.slot_ref, s32[3]{0:T(128)} %and_select_fusion.5.tile_ref.source_ref, s32[3]{0:T(128)} %and_select_fusion.5.tile_ref.source_ref, ...), custom_call_target="tpu_custom_call", output_to_operand_aliasing={{0}: (9, {}), {1}: (10, {})} | custom-call | flops 1811939328 | bytes 8257536 | tf_op jit(solution)/shard_map/pallas_call | solution.py:77
  42.1 7.1 %shard_map.87 = (bf16[16,256,512]{2,1,0:T(8,128)(2,1)}, bf16[16,256,512]{2,1,0:T(8,128)(2,1)}, f32[384,512]{1,0:T(8,128)}) custom-call(s32[3]{0:T(128)} %get-tuple-element.270.slot_ref, s32[3]{0:T(128)} %and_select_fusion.4.tile_ref.source_ref, s32[3]{0:T(128)} %and_select_fusion.4.tile_ref.source_ref, ...), custom_call_target="tpu_custom_call", output_to_operand_aliasing={{0}: (9, {}), {1}: (10, {})} | custom-call | flops 1811939328 | bytes 8257536 | tf_op jit(solution)/shard_map/pallas_call | solution.py:77
  50.5 4.6 %collective-permute-done.3 = bf16[4,64,512]{2,1,0:T(8,128)(2,1)S(1)} collective-permute-done((bf16[4,64,512]{2,1,0:T(8,128)(2,1)S(1)}, bf16[4,64,512]{2,1,0:T(8,128)(2,1)S(1)}, u32[]{:S(2)}, u32[]{:S(2)}) %collective-permute-start.3) | collective-permute-done | bytes 262176 | tf_op jit(solution)/shard_map/ppermute | solution.py:89
  55.4 7.1 %shard_map.88 = (bf16[16,256,512]{2,1,0:T(8,128)(2,1)}, bf16[16,256,512]{2,1,0:T(8,128)(2,1)}, f32[384,512]{1,0:T(8,128)}) custom-call(s32[3]{0:T(128)} %get-tuple-element.271.slot_ref, s32[3]{0:T(128)} %and_select_fusion.3.tile_ref.source_ref, s32[3]{0:T(128)} %and_select_fusion.3.tile_ref.source_ref, ...), custom_call_target="tpu_custom_call", output_to_operand_aliasing={{0}: (9, {}), {1}: (10, {})} | custom-call | flops 1811939328 | bytes 8257536 | tf_op jit(solution)/shard_map/pallas_call | solution.py:77
  67.6 7.1 %shard_map.89 = (bf16[16,256,512]{2,1,0:T(8,128)(2,1)}, bf16[16,256,512]{2,1,0:T(8,128)(2,1)}, f32[384,512]{1,0:T(8,128)}) custom-call(s32[3]{0:T(128)} %get-tuple-element.272.slot_ref, s32[3]{0:T(128)} %and_select_fusion.2.tile_ref.source_ref, s32[3]{0:T(128)} %and_select_fusion.2.tile_ref.source_ref, ...), custom_call_target="tpu_custom_call", output_to_operand_aliasing={{0}: (9, {}), {1}: (10, {})} | custom-call | flops 1811939328 | bytes 8257536 | tf_op jit(solution)/shard_map/pallas_call | solution.py:77
  77.1 2.9 %collective-permute-start.9 = (bf16[4,64,512]{2,1,0:T(8,128)(2,1)S(1)}, bf16[4,64,512]{2,1,0:T(8,128)(2,1)S(1)}, u32[]{:S(2)}, u32[]{:S(2)}) collective-permute-start(bf16[4,64,512]{2,1,0:T(8,128)(2,1)S(1)} %pad_maximum_fusion.6), channel_id=1, source_target_pairs={{0,4},{1,5},{2,6},{3,7},{4,0},{5,1},{6,2},{7,3},{8,12},{9,13},{10,... | collective-permute-start | bytes 786440 | tf_op jit(solution)/shard_map/ppermute | solution.py:89
  80.0 5.8 %shard_map.90 = (bf16[16,256,512]{2,1,0:T(8,128)(2,1)}, bf16[16,256,512]{2,1,0:T(8,128)(2,1)}, f32[384,512]{1,0:T(8,128)}) custom-call(s32[2]{0:T(128)} %get-tuple-element.274.slot_ref, s32[2]{0:T(128)} %and_select_fusion.1.tile_ref.source_ref, s32[2]{0:T(128)} %and_select_fusion.1.tile_ref.source_ref, ...), custom_call_target="tpu_custom_call", output_to_operand_aliasing={{0}: (9, {}), {1}: (10, {})} | custom-call | flops 1207959552 | bytes 6291456 | tf_op jit(solution)/shard_map/pallas_call | solution.py:77
  85.9 4.6 %collective-permute-done.9 = bf16[4,64,512]{2,1,0:T(8,128)(2,1)S(1)} collective-permute-done((bf16[4,64,512]{2,1,0:T(8,128)(2,1)S(1)}, bf16[4,64,512]{2,1,0:T(8,128)(2,1)S(1)}, u32[]{:S(2)}, u32[]{:S(2)}) %collective-permute-start.9) | collective-permute-done | bytes 262176 | tf_op jit(solution)/shard_map/ppermute | solution.py:89
  92.4 10.2 %collective-permute-done.11 = bf16[4,128,512]{2,1,0:T(8,128)(2,1)S(1)} collective-permute-done((bf16[4,128,512]{2,1,0:T(8,128)(2,1)S(1)}, bf16[4,128,512]{2,1,0:T(8,128)(2,1)S(1)}, u32[]{:S(2)}, u32[]{:S(2)}) %collective-permute-start.11) | collective-permute-done | bytes 524320 | tf_op jit(solution)/shard_map/ppermute | solution.py:89
  104.8 5.8 %shard_map.91 = (bf16[16,256,512]{2,1,0:T(8,128)(2,1)}, bf16[16,256,512]{2,1,0:T(8,128)(2,1)}, f32[384,512]{1,0:T(8,128)}) custom-call(s32[2]{0:T(128)} %get-tuple-element.275.slot_ref, s32[2]{0:T(128)} %broadcast_select_fusion.13.tile_ref, s32[2]{0:T(128)} %broadcast_select_fusion.12.source_ref, ...), custom_call_target="tpu_custom_call", output_to_operand_aliasing={{0}: (9, {}), {1}: (10, {})} | custom-call | flops 1207959552 | bytes 6291456 | tf_op jit(solution)/shard_map/pallas_call | solution.py:77
  110.5 3.8 %fusion.106 = (bf16[16,64,512]{2,1,0:T(8,128)(2,1)S(1)}, bf16[16,64,512]{2,1,0:T(8,128)(2,1)S(1)}, bf16[16,64,512]{2,1,0:T(8,128)(2,1)}, bf16[16,64,512]{2,1,0:T(8,128)(2,1)S(1)}) fusion(bf16[16,256,512]{2,1,0:T(8,128)(2,1)} %get-tuple-element.69), kind=kLoop, calls=%fused_computation.389 | loop fusion | bytes 8388608 | tf_op jit(solution)/shard_map/slice | solution.py:220
  115.3 3.0 %fusion.62 = (f32[2,2,64,512]{3,2,1,0:T(8,128)S(1)}, f32[2,2,64,512]{3,2,1,0:T(8,128)S(1)}, f32[2,2,64,512]{3,2,1,0:T(8,128)S(1)}, f32[2,2,64,512]{3,2,1,0:T(8,1...) fusion(pred[2,2,2]{2,1,0:T(4,128)(4,1)S(1)} %bitcast.535, ...), kind=kLoop, calls=%fused_computation.144 | loop fusion | flops 7340032 | bytes 10485832 | tf_op jit(solution)/shard_map/reduce_sum | solution.py:100
  122.5 3.0 %fusion.66 = (f32[2,2,64,512]{3,2,1,0:T(8,128)S(1)}, f32[2,2,64,512]{3,2,1,0:T(8,128)S(1)}, f32[2,2,64,512]{3,2,1,0:T(8,128)S(1)}, f32[2,2,64,512]{3,2,1,0:T(8,1...) fusion(pred[2,2,2]{2,1,0:T(4,128)(4,1)S(1)} %bitcast.527, ...), kind=kLoop, calls=%fused_computation.148 | loop fusion | flops 7340032 | bytes 10485832 | tf_op jit(solution)/shard_map/reduce_sum | solution.py:100
  127.6 2.8 %fusion.34 = (f32[2,2,2,32,512]{4,3,2,1,0:T(8,128)S(1)}, f32[2,2,2,32,512]{4,3,2,1,0:T(8,128)S(1)}, f32[2,2,2,32,512]{4,3,2,1,0:T(8,128)S(1)}, f32[2,2,2,32,512]...) fusion(pred[2,2,2,2]{3,2,1,0:T(4,128)(4,1)S(1)} %get-tuple-elem, ...), kind=kLoop, calls=%fused_computation.116 | loop fusion | flops 7340032 | bytes 10485832 | tf_op jit(solution)/shard_map/reduce_sum | solution.py:100
  138.3 14.0 %collective-permute-done.29 = bf16[2,2,4,64,512]{4,3,2,0,1:T(8,128)(2,1)S(1)} collective-permute-done((bf16[2,2,4,64,512]{4,3,2,0,1:T(8,128)(2,1)S(1)}, bf16[2,2,4,64,512]{4,3,2,0,1:T(8,128)(2,1)S(1)}, u32[]{:S(2)}, u32[]{:S(2)}) %collective-permute-start.29) | collective-permute-done | bytes 1048608 | tf_op jit(solution)/shard_map/ppermute | solution.py:89
  159.1 15.6 %collective-permute-done.19 = bf16[2,2,4,64,512]{4,3,2,0,1:T(8,128)(2,1)S(1)} collective-permute-done((bf16[2,2,4,64,512]{4,3,2,0,1:T(8,128)(2,1)S(1)}, bf16[2,2,4,64,512]{4,3,2,0,1:T(8,128)(2,1)S(1)}, u32[]{:S(2)}, u32[]{:S(2)}) %collective-permute-start.19) | collective-permute-done | bytes 1048608 | tf_op jit(solution)/shard_map/ppermute | solution.py:89
  181.6 9.5 %collective-permute-done.30 = bf16[2,2,4,32,512]{4,3,2,0,1:T(8,128)(2,1)} collective-permute-done((bf16[2,2,4,32,512]{4,3,2,0,1:T(8,128)(2,1)}, bf16[2,2,4,32,512]{4,3,2,0,1:T(8,128)(2,1)}, u32[]{:S(2)}, u32[]{:S(2)}) %collective-permute-start.30) | collective-permute-done | bytes 524320 | tf_op jit(solution)/shard_map/ppermute | solution.py:89
  195.9 5.2 %collective-permute-done.20 = bf16[2,2,4,32,512]{4,3,2,0,1:T(8,128)(2,1)} collective-permute-done((bf16[2,2,4,32,512]{4,3,2,0,1:T(8,128)(2,1)}, bf16[2,2,4,32,512]{4,3,2,0,1:T(8,128)(2,1)}, u32[]{:S(2)}, u32[]{:S(2)}) %collective-permute-start.20) | collective-permute-done | bytes 524320 | tf_op jit(solution)/shard_map/ppermute | solution.py:89
  208.8 8.4 %collective-permute-done.21 = bf16[2,4,32,512]{3,2,1,0:T(8,128)(2,1)S(1)} collective-permute-done((bf16[2,4,32,512]{3,2,1,0:T(8,128)(2,1)S(1)}, bf16[2,4,32,512]{3,2,1,0:T(8,128)(2,1)S(1)}, u32[]{:S(2)}, u32[]{:S(2)}) %collective-permute-start.21) | collective-permute-done | bytes 262176 | tf_op jit(solution)/shard_map/ppermute | solution.py:89
  218.2 3.5 %collective-permute-done.16 = bf16[2,4,32,512]{3,2,0,1:T(8,128)(2,1)S(1)} collective-permute-done((bf16[2,4,32,512]{3,2,0,1:T(8,128)(2,1)S(1)}, bf16[2,4,32,512]{3,2,0,1:T(8,128)(2,1)S(1)}, u32[]{:S(2)}, u32[]{:S(2)}) %collective-permute-start.16) | collective-permute-done | bytes 262176 | tf_op jit(solution)/shard_map/ppermute | solution.py:89
  222.2 8.5 %collective-permute-done.22 = bf16[4,32,512]{2,1,0:T(8,128)(2,1)S(1)} collective-permute-done((bf16[4,32,512]{2,1,0:T(8,128)(2,1)S(1)}, bf16[4,32,512]{2,1,0:T(8,128)(2,1)S(1)}, u32[]{:S(2)}, u32[]{:S(2)}) %collective-permute-start.22) | collective-permute-done | bytes 131104 | tf_op jit(solution)/shard_map/ppermute | solution.py:89
  234.9 19.9 %all-gather.2.cloned.1.call-done = bf16[4,4,128,512]{3,2,1,0:T(8,128)(2,1)} async-done(((bf16[1,4,128,512]{3,2,1,0:T(8,128)(2,1)}), bf16[4,4,128,512]{3,2,1,0:T(8,128)(2,1)}) %all-gather.2.cloned.1.call-update) | async-done | bytes 2097168 | tf_op jit(solution)/shard_map/all_gather | solution.py:225
  258.9 3.0 %fusion.1 = f32[2048,512]{1,0:T(8,128)} fusion(f32[2048,512]{1,0:T(8,128)S(1)} %copy-done.2, bf16[4,2,256,512]{3,2,1,0:T(8,128)(2,1)S(1)} %pad_maximum_fusion.1), kind=kLoop, calls=%fused_computation.9 | loop fusion | flops 5242880 | bytes 10485760 | tf_op jit(solution)/shard_map/sub | solution.py:236
  (236 shorter events, 87.7 us)
Async XLA Ops:
  7.2 247.7 %all-gather.2.cloned.1.call-start = ((), (), s32[]{:S(2)}) async-start(), calls=%async_computation | async-start | bytes 2621440 | tf_op jit(solution)/shard_map/all_gather | solution.py:225
  9.9 27.6 %collective-permute-start = (bf16[4,128,512]{2,1,0:T(8,128)(2,1)S(1)}, bf16[4,128,512]{2,1,0:T(8,128)(2,1)}, u32[]{:S(2)}, u32[]{:S(2)}) collective-permute-start(bf16[4,128,512]{2,1,0:T(8,128)(2,1)S(1)} %constant_dynamic-slice_fusion.9), channel_id=1, source_target_pairs={{0,1},{1,0},{2,3},{3,2},{4,5},{5,4},{6,7},{7,6},{8,9},{9,8},{10,11... | collective-permute-start | bytes 1572872 | tf_op jit(solution)/shard_map/ppermute | solution.py:89
  13.0 24.7 %collective-permute-start.1 = (bf16[4,128,512]{2,1,0:T(8,128)(2,1)S(1)}, bf16[4,128,512]{2,1,0:T(8,128)(2,1)}, u32[]{:S(2)}, u32[]{:S(2)}) collective-permute-start(bf16[4,128,512]{2,1,0:T(8,128)(2,1)S(1)} %constant_dynamic-slice_fusion.8), channel_id=1, source_target_pairs={{0,2},{1,3},{2,0},{3,1},{4,6},{5,7},{6,4},{7,5},{8,10},{9,11},{10,... | collective-permute-start | bytes 1572872 | tf_op jit(solution)/shard_map/ppermute | solution.py:89
  15.0 76.1 %collective-permute-start.12 = (s32[16]{0:T(128)S(1)}, s32[16]{0:T(128)S(1)}, u32[]{:S(2)}, u32[]{:S(2)}) collective-permute-start(s32[16]{0:T(128)S(1)} %get-tuple-element.260), channel_id=1, source_target_pairs={{0,8},{8,0},{16,24},{24,16},{1,9},{9,1},{17,25},{25,17},{2,10},{10... | collective-permute-start | bytes 200 | tf_op jit(solution)/shard_map/ppermute | solution.py:89
  37.9 12.6 %collective-permute-start.2 = (bf16[4,64,512]{2,1,0:T(8,128)(2,1)S(1)}, bf16[4,64,512]{2,1,0:T(8,128)(2,1)S(1)}, u32[]{:S(2)}, u32[]{:S(2)}) collective-permute-start(bf16[4,64,512]{2,1,0:T(8,128)(2,1)S(1)} %constant_dynamic-slice_fusion.7), channel_id=1, source_target_pairs={{0,2},{1,3},{2,0},{3,1},{4,6},{5,7},{6,4},{7,5},{8,10},{9,11},{10,... | collective-permute-start | bytes 786440 | tf_op jit(solution)/shard_map/ppermute | solution.py:89
  39.4 15.7 %collective-permute-start.3 = (bf16[4,64,512]{2,1,0:T(8,128)(2,1)S(1)}, bf16[4,64,512]{2,1,0:T(8,128)(2,1)S(1)}, u32[]{:S(2)}, u32[]{:S(2)}) collective-permute-start(bf16[4,64,512]{2,1,0:T(8,128)(2,1)S(1)} %constant_dynamic-slice_fusion.6), channel_id=1, source_target_pairs={{0,4},{1,5},{2,6},{3,7},{4,0},{5,1},{6,2},{7,3},{8,12},{9,13},{10,... | collective-permute-start | bytes 786440 | tf_op jit(solution)/shard_map/ppermute | solution.py:89
  77.1 13.3 %collective-permute-start.9 = (bf16[4,64,512]{2,1,0:T(8,128)(2,1)S(1)}, bf16[4,64,512]{2,1,0:T(8,128)(2,1)S(1)}, u32[]{:S(2)}, u32[]{:S(2)}) collective-permute-start(bf16[4,64,512]{2,1,0:T(8,128)(2,1)S(1)} %pad_maximum_fusion.6), channel_id=1, source_target_pairs={{0,4},{1,5},{2,6},{3,7},{4,0},{5,1},{6,2},{7,3},{8,12},{9,13},{10,... | collective-permute-start | bytes 786440 | tf_op jit(solution)/shard_map/ppermute | solution.py:89
  90.5 12.1 %collective-permute-start.11 = (bf16[4,128,512]{2,1,0:T(8,128)(2,1)S(1)}, bf16[4,128,512]{2,1,0:T(8,128)(2,1)S(1)}, u32[]{:S(2)}, u32[]{:S(2)}) collective-permute-start(bf16[4,128,512]{2,1,0:T(8,128)(2,1)S(1)} %pad_maximum_fusion.3), channel_id=1, source_target_pairs={{0,2},{1,3},{2,0},{3,1},{4,6},{5,7},{6,4},{7,5},{8,10},{9,11},{10,... | collective-permute-start | bytes 1572872 | tf_op jit(solution)/shard_map/ppermute | solution.py:89
  91.2 12.0 %collective-permute-start.10 = (bf16[4,128,512]{2,1,0:T(8,128)(2,1)S(1)}, bf16[4,128,512]{2,1,0:T(8,128)(2,1)S(1)}, u32[]{:S(2)}, u32[]{:S(2)}) collective-permute-start(bf16[4,128,512]{2,1,0:T(8,128)(2,1)S(1)} %pad_maximum_fusion.2), channel_id=1, source_target_pairs={{0,1},{1,0},{2,3},{3,2},{4,5},{5,4},{6,7},{7,6},{8,9},{9,8},{10,11... | collective-permute-start | bytes 1572872 | tf_op jit(solution)/shard_map/ppermute | solution.py:89
  126.2 26.1 %collective-permute-start.29 = (bf16[2,2,4,64,512]{4,3,2,0,1:T(8,128)(2,1)S(1)}, bf16[2,2,4,64,512]{4,3,2,0,1:T(8,128)(2,1)S(1)}, u32[]{:S(2)}, u32[]{:S(2)}) collective-permute-start(bf16[2,2,4,64,512]{4,3,2,0,1:T(8,128)(2,1)S(1)} %fusion.5), channel_id=1, source_target_pairs={{0,1},{1,0},{2,3},{3,2},{4,5},{5,4},{6,7},{7,6},{8,9},{9,8},{10,11... | collective-permute-start | bytes 3145736 | tf_op jit(solution)/shard_map/ppermute | solution.py:89
  131.1 26.1 %collective-permute-start.24 = (bf16[2,2,2,4,32,512]{5,4,3,0,1,2:T(8,128)(2,1)S(1)}, bf16[2,2,2,4,32,512]{5,4,3,0,1,2:T(8,128)(2,1)S(1)}, u32[]{:S(2)}, u32[]{:S(2)}) collective-permute-start(bf16[2,2,2,4,32,512]{5,4,3,0,1,2:T(8,128)(2,1)S(1)} %fusion.4), channel_id=1, source_target_pairs={{0,16},{8,24},{16,0},{24,8},{1,17},{9,25},{17,1},{25,9},{2,18},{10... | collective-permute-start | bytes 3145736 | tf_op jit(solution)/shard_map/ppermute | solution.py:89
  132.3 42.4 %collective-permute-start.19 = (bf16[2,2,4,64,512]{4,3,2,0,1:T(8,128)(2,1)S(1)}, bf16[2,2,4,64,512]{4,3,2,0,1:T(8,128)(2,1)S(1)}, u32[]{:S(2)}, u32[]{:S(2)}) collective-permute-start(bf16[2,2,4,64,512]{4,3,2,0,1:T(8,128)(2,1)S(1)} %fusion.3), channel_id=1, source_target_pairs={{0,1},{1,0},{2,3},{3,2},{4,5},{5,4},{6,7},{7,6},{8,9},{9,8},{10,11... | collective-permute-start | bytes 3145736 | tf_op jit(solution)/shard_map/ppermute | solution.py:89
  134.9 44.8 %collective-permute-start.14 = (bf16[2,2,2,4,32,512]{5,4,2,1,0,3:T(8,128)(2,1)S(1)}, bf16[2,2,2,4,32,512]{5,4,2,1,0,3:T(8,128)(2,1)S(1)}, u32[]{:S(2)}, u32[]{:S(2)}) collective-permute-start(bf16[2,2,2,4,32,512]{5,4,2,1,0,3:T(8,128)(2,1)S(1)} %fusion.2), channel_id=1, source_target_pairs={{0,16},{8,24},{16,0},{24,8},{1,17},{9,25},{17,1},{25,9},{2,18},{10... | collective-permute-start | bytes 3145736 | tf_op jit(solution)/shard_map/ppermute | solution.py:89
  153.8 37.3 %collective-permute-start.30 = (bf16[2,2,4,32,512]{4,3,2,0,1:T(8,128)(2,1)}, bf16[2,2,4,32,512]{4,3,2,0,1:T(8,128)(2,1)}, u32[]{:S(2)}, u32[]{:S(2)}) collective-permute-start(bf16[2,2,4,32,512]{4,3,2,0,1:T(8,128)(2,1)} %get-tuple-element.208), channel_id=1, source_target_pairs={{0,16},{8,24},{16,0},{24,8},{1,17},{9,25},{17,1},{25,9},{2,18},{10... | collective-permute-start | bytes 1572872 | tf_op jit(solution)/shard_map/ppermute | solution.py:89
  158.4 36.0 %collective-permute-start.25 = (bf16[2,2,4,32,512]{4,3,2,0,1:T(8,128)(2,1)}, bf16[2,2,4,32,512]{4,3,2,0,1:T(8,128)(2,1)}, u32[]{:S(2)}, u32[]{:S(2)}) collective-permute-start(bf16[2,2,4,32,512]{4,3,2,0,1:T(8,128)(2,1)} %get-tuple-element.206), channel_id=1, source_target_pairs={{0,1},{1,0},{2,3},{3,2},{4,5},{5,4},{6,7},{7,6},{8,9},{9,8},{10,11... | collective-permute-start | bytes 1572872 | tf_op jit(solution)/shard_map/ppermute | solution.py:89
  175.9 25.2 %collective-permute-start.20 = (bf16[2,2,4,32,512]{4,3,2,0,1:T(8,128)(2,1)}, bf16[2,2,4,32,512]{4,3,2,0,1:T(8,128)(2,1)}, u32[]{:S(2)}, u32[]{:S(2)}) collective-permute-start(bf16[2,2,4,32,512]{4,3,2,0,1:T(8,128)(2,1)} %get-tuple-element.204), channel_id=1, source_target_pairs={{0,16},{8,24},{16,0},{24,8},{1,17},{9,25},{17,1},{25,9},{2,18},{10... | collective-permute-start | bytes 1572872 | tf_op jit(solution)/shard_map/ppermute | solution.py:89
  180.8 23.3 %collective-permute-start.15 = (bf16[2,2,4,32,512]{4,3,1,0,2:T(8,128)(2,1)}, bf16[2,2,4,32,512]{4,3,1,0,2:T(8,128)(2,1)}, u32[]{:S(2)}, u32[]{:S(2)}) collective-permute-start(bf16[2,2,4,32,512]{4,3,1,0,2:T(8,128)(2,1)} %get-tuple-element.202), channel_id=1, source_target_pairs={{0,1},{1,0},{2,3},{3,2},{4,5},{5,4},{6,7},{7,6},{8,9},{9,8},{10,11... | collective-permute-start | bytes 1572872 | tf_op jit(solution)/shard_map/ppermute | solution.py:89
  192.6 13.1 %collective-permute-start.31 = (bf16[2,4,32,512]{3,2,1,0:T(8,128)(2,1)S(1)}, bf16[2,4,32,512]{3,2,1,0:T(8,128)(2,1)S(1)}, u32[]{:S(2)}, u32[]{:S(2)}) collective-permute-start(bf16[2,4,32,512]{3,2,1,0:T(8,128)(2,1)S(1)} %get-tuple-element.222), channel_id=1, source_target_pairs={{0,2},{1,3},{2,0},{3,1},{4,6},{5,7},{6,4},{7,5},{8,10},{9,11},{10,... | collective-permute-start | bytes 786440 | tf_op jit(solution)/shard_map/ppermute | solution.py:89
  195.6 11.8 %collective-permute-start.26 = (bf16[2,4,32,512]{3,2,1,0:T(8,128)(2,1)S(1)}, bf16[2,4,32,512]{3,2,1,0:T(8,128)(2,1)S(1)}, u32[]{:S(2)}, u32[]{:S(2)}) collective-permute-start(bf16[2,4,32,512]{3,2,1,0:T(8,128)(2,1)S(1)} %get-tuple-element.220), channel_id=1, source_target_pairs={{0,2},{1,3},{2,0},{3,1},{4,6},{5,7},{6,4},{7,5},{8,10},{9,11},{10,... | collective-permute-start | bytes 786440 | tf_op jit(solution)/shard_map/ppermute | solution.py:89
  202.3 14.9 %collective-permute-start.21 = (bf16[2,4,32,512]{3,2,1,0:T(8,128)(2,1)S(1)}, bf16[2,4,32,512]{3,2,1,0:T(8,128)(2,1)S(1)}, u32[]{:S(2)}, u32[]{:S(2)}) collective-permute-start(bf16[2,4,32,512]{3,2,1,0:T(8,128)(2,1)S(1)} %get-tuple-element.218), channel_id=1, source_target_pairs={{0,2},{1,3},{2,0},{3,1},{4,6},{5,7},{6,4},{7,5},{8,10},{9,11},{10,... | collective-permute-start | bytes 786440 | tf_op jit(solution)/shard_map/ppermute | solution.py:89
  205.3 16.3 %collective-permute-start.16 = (bf16[2,4,32,512]{3,2,0,1:T(8,128)(2,1)S(1)}, bf16[2,4,32,512]{3,2,0,1:T(8,128)(2,1)S(1)}, u32[]{:S(2)}, u32[]{:S(2)}) collective-permute-start(bf16[2,4,32,512]{3,2,0,1:T(8,128)(2,1)S(1)} %get-tuple-element.216), channel_id=1, source_target_pairs={{0,2},{1,3},{2,0},{3,1},{4,6},{5,7},{6,4},{7,5},{8,10},{9,11},{10,... | collective-permute-start | bytes 786440 | tf_op jit(solution)/shard_map/ppermute | solution.py:89
  205.7 16.4 %collective-permute-start.32 = (bf16[4,32,512]{2,1,0:T(8,128)(2,1)S(1)}, bf16[4,32,512]{2,1,0:T(8,128)(2,1)S(1)}, u32[]{:S(2)}, u32[]{:S(2)}) collective-permute-start(bf16[4,32,512]{2,1,0:T(8,128)(2,1)S(1)} %fusion.93), channel_id=1, source_target_pairs={{0,4},{1,5},{2,6},{3,7},{4,0},{5,1},{6,2},{7,3},{8,12},{9,13},{10,... | collective-permute-start | bytes 393224 | tf_op jit(solution)/shard_map/ppermute | solution.py:89
  207.5 14.7 %collective-permute-start.27 = (bf16[4,32,512]{2,1,0:T(8,128)(2,1)S(1)}, bf16[4,32,512]{2,1,0:T(8,128)(2,1)S(1)}, u32[]{:S(2)}, u32[]{:S(2)}) collective-permute-start(bf16[4,32,512]{2,1,0:T(8,128)(2,1)S(1)} %fusion.91), channel_id=1, source_target_pairs={{0,4},{1,5},{2,6},{3,7},{4,0},{5,1},{6,2},{7,3},{8,12},{9,13},{10,... | collective-permute-start | bytes 393224 | tf_op jit(solution)/shard_map/ppermute | solution.py:89
  217.3 13.5 %collective-permute-start.22 = (bf16[4,32,512]{2,1,0:T(8,128)(2,1)S(1)}, bf16[4,32,512]{2,1,0:T(8,128)(2,1)S(1)}, u32[]{:S(2)}, u32[]{:S(2)}) collective-permute-start(bf16[4,32,512]{2,1,0:T(8,128)(2,1)S(1)} %fusion.89), channel_id=1, source_target_pairs={{0,4},{1,5},{2,6},{3,7},{4,0},{5,1},{6,2},{7,3},{8,12},{9,13},{10,... | collective-permute-start | bytes 393224 | tf_op jit(solution)/shard_map/ppermute | solution.py:89
  (16 other events, 141.6 us)
Sparse Core Ops, SparseCore 0:
  233.9 20.8 all-gather.1
